TPU v7x, 768 devices: a whole 4x8x12 slice. The times are simulated.
768 devices in a mesh: blk: 48 (over z_hi, y, core), dp: 16 (over x, z_lo).
Axes of the slice: x: 4, y: 8, z: 12 (z_hi: 3, z_lo: 4; z = z_hi * 4 + z_lo), core: 2. Of those that a mesh axis runs over, the one named last changes fastest.
Arguments:
- visual_encodings: bfloat16 [98304, 1152], P(('blk', 'dp')), may hold values from -0.1875 to 0.1875
- sentence_descriptors_prelift: bfloat16 [98304, 1152], P(('blk', 'dp')), may hold values from -0.75 to 0.75
- partner_global_rows: int32 [98304], P(('blk', 'dp')), may hold values from 0 to 98303, as said below
- sentence_lifting_weights: bfloat16 [1152, 1152], replicated, may hold values from -0.1875 to 0.1875
- lifting_perturbation: bfloat16 [1152, 1152], replicated, may hold values from -0.09375 to 0.09375
- logit_scaling_value: float32 [], replicated, may hold values from 2 to 8
- logit_additive_bias: float32 [], replicated, may hold values from -3 to 0
Outputs:
- image_grad: bfloat16 [98304, 1152], P(('blk', 'dp'))
- text_grad: bfloat16 [98304, 1152], P(('blk', 'dp'))
- head_grad: float32 [1152, 576], P('blk', 'dp')
Inputs may be any that keep to these rules, and one draw needn't show every extreme that they name: `partner_global_rows`: the text row in block (b, d) names an image row of block ((b + k) mod 48, d) with k 0 or 1.
All inputs are finite; a program needn't handle non-finite values.
Results may differ from a plain program's by a relative error of at most 0.011.
Values may be sent and summed in bfloat16 or wider, within the bound.
A program may use at most 32 MiB of HBM per device.

v0:
```python
import jax
import jax.numpy as jnp
from jax import lax
from jax.sharding import PartitionSpec as P

HEAD_COLS = 576


EPSILON = 1e-06


def shifted(block, axis, distance):
    devices = range(lax.axis_size(axis))
    route = [((i - distance) % len(devices), i) for i in devices]
    return lax.ppermute(block, axis, route)


def sigmoidal_scale_portion(
    visual_direction_vector,
    picture_entry_span,
    caption_unit_length,
    caption_match,
    logit_scaling_value,
    logit_additive_bias,
):
    angular_closeness_table = (
        logit_scaling_value
        * lax.dot_general(
            visual_direction_vector,
            caption_unit_length,
            (((1,), (1,)), ((), ())),
            preferred_element_type=jnp.float32,
        )
        + logit_additive_bias
    )
    label_sign = jnp.where(caption_match[None, :] == picture_entry_span[:, None], 1.0, -1.0).astype(
        jnp.float32
    )
    return (-label_sign * jax.nn.sigmoid(-label_sign * angular_closeness_table)).astype(
        jnp.bfloat16
    )


def flipped_operand_contraction(left, right):
    return lax.dot_general(
        left, right, (((0,), (0,)), ((), ())), preferred_element_type=jnp.float32
    )


def shards(
    visual_encodings,
    sentence_descriptors_prelift,
    partner_global_rows,
    sentence_lifting_weights,
    lifting_perturbation,
    logit_scaling_value,
    logit_additive_bias,
):
    piece_list = visual_encodings.shape[0]
    perturbed = (
        sentence_lifting_weights.astype(jnp.float32) + lifting_perturbation.astype(jnp.float32)
    ).astype(jnp.bfloat16)
    projected = jnp.dot(sentence_descriptors_prelift, perturbed, preferred_element_type=jnp.float32)
    text_scale = lax.rsqrt(jnp.sum(projected * projected, axis=1, keepdims=True) + EPSILON)
    caption_unit_length = (projected * text_scale).astype(jnp.bfloat16)
    image_float = visual_encodings.astype(jnp.float32)
    image_scale = lax.rsqrt(jnp.sum(image_float * image_float, axis=1, keepdims=True) + EPSILON)
    visual_direction_vector = (image_float * image_scale).astype(jnp.bfloat16)
    group_size = lax.axis_size("dp")
    cycle_place = lax.axis_index("blk")
    data_group = lax.axis_index("dp")
    shard_lines = jnp.arange(piece_list, dtype=jnp.int32)
    current_entry_span = (cycle_place * group_size + data_group) * piece_list + shard_lines
    present_coefficient_value = sigmoidal_scale_portion(
        visual_direction_vector,
        current_entry_span,
        caption_unit_length,
        partner_global_rows,
        logit_scaling_value,
        logit_additive_bias,
    )
    incoming_caption, incoming_matches = shifted(
        (caption_unit_length, partner_global_rows), "blk", 1
    )
    former_round_coefficient = sigmoidal_scale_portion(
        visual_direction_vector,
        current_entry_span,
        incoming_caption,
        incoming_matches,
        logit_scaling_value,
        logit_additive_bias,
    )
    visual_direction_sensitivity = logit_scaling_value * (
        jnp.dot(present_coefficient_value, caption_unit_length, preferred_element_type=jnp.float32)
        + jnp.dot(former_round_coefficient, incoming_caption, preferred_element_type=jnp.float32)
    )
    present_sensitivity = logit_scaling_value * flipped_operand_contraction(
        present_coefficient_value, visual_direction_vector
    )
    former_round_sensitivity = logit_scaling_value * flipped_operand_contraction(
        former_round_coefficient, visual_direction_vector
    )
    returned = shifted(former_round_sensitivity, "blk", -1)
    unit_text_grad = present_sensitivity + returned
    image_dir = image_float * image_scale
    image_grad = (
        image_scale
        * (
            visual_direction_sensitivity
            - image_dir * jnp.sum(image_dir * visual_direction_sensitivity, axis=1, keepdims=True)
        )
    ).astype(jnp.bfloat16)
    text_dir = projected * text_scale
    pre_grad = (
        text_scale
        * (unit_text_grad - text_dir * jnp.sum(text_dir * unit_text_grad, axis=1, keepdims=True))
    ).astype(jnp.bfloat16)
    text_grad = lax.dot_general(
        pre_grad, perturbed, (((1,), (1,)), ((), ())), preferred_element_type=jnp.float32
    ).astype(jnp.bfloat16)
    head_part = pre_grad[:, :HEAD_COLS]
    cycle_part = lax.psum_scatter(
        flipped_operand_contraction(sentence_descriptors_prelift, head_part),
        "blk",
        scatter_dimension=0,
        tiled=True,
    )
    head_grad = lax.psum_scatter(cycle_part, "dp", scatter_dimension=1, tiled=True)
    return (image_grad, text_grad, head_grad)


def solution(mesh):
    in_specs = (
        P(("blk", "dp"), None),
        P(("blk", "dp"), None),
        P(("blk", "dp")),
        P(),
        P(),
        P(),
        P(),
    )
    out_specs = (P(("blk", "dp"), None), P(("blk", "dp"), None), P("blk", "dp"))
    return jax.shard_map(shards, mesh=mesh, in_specs=in_specs, out_specs=out_specs, check_vma=False)
```

profile of v0, /device:TPU:66, one launch (start us, length us, event | category | flops | bytes accessed | tf_op | source)
XLA Modules:
  0.0 656.5 jit_solution(17534799568972747957)
XLA Ops:
  7.2 0.9 copy-done
  8.1 3.5 multiply_reduce_fusion
  11.7 1.9 collective-permute-start.1
  13.6 3.6 collective-permute-start
  18.9 16.6 %collective-permute-done = s32[128]{0:T(128)S(1)} collective-permute-done((s32[128]{0:T(128)S(1)}, s32[128]{0:T(128)S(1)}, u32[]{:S(2)}, u32[]{:S(2)}) %collective-permute-start) | collective-permute-done | bytes 544 | tf_op jit(solution)/shard_map/ppermute | solution.py:15
  36.5 1.9 collective-permute-start.2
  38.8 11.9 %collective-permute-done.2 = f32[128,1152]{0,1:T(8,128)S(1)} collective-permute-done((f32[128,1152]{0,1:T(8,128)S(1)}, f32[128,1152]{0,1:T(8,128)S(1)}, u32[]{:S(2)}, u32[]{:S(2)}) %collective-permute-start.2) | collective-permute-done | bytes 589856 | tf_op jit(solution)/shard_map/ppermute | solution.py:15
  51.1 2.0 convolution_bitcast_fusion
  53.1 1.3 dynamic-slice.6
  54.4 1.3 dynamic-slice
  57.0 1.4 fusion.37
  58.4 1.3 fusion.23
  59.7 0.8 fusion.26
  60.5 1.8 copy.22
  62.4 522.7 %all-reduce.5.cloned.1.call-done = f32[1152,576]{0,1:T(8,128)} async-done(((f32[1152,576]{0,1:T(8,128)}), f32[1152,576]{0,1:T(8,128)}) %all-reduce.5.cloned.1.call-update) | async-done | bytes 2654224
  585.1 1.2 constant_dynamic-slice_fusion.1
  586.3 39.3 %fusion = f32[24,48]{0,1:T(8,128)} fusion(f32[24,576]{0,1:T(8,128)S(1)} %constant_dynamic-slice_fusion.1), kind=kCustom, calls=%all-reduce-scatter | all-reduce-scatter fusion | flops 18433 | bytes 64000
  625.5 0.7 slice.5
  626.3 5.5 collective-permute-start.5
  631.8 1.9 collective-permute-start.4
  633.7 3.4 collective-permute-start.3
  637.1 7.8 %collective-permute-start.6 = (f32[24,36]{0,1:T(8,128)S(1)}, f32[24,36]{0,1:T(8,128)S(1)}, u32[]{:S(2)}, u32[]{:S(2)}) collective-permute-start(f32[24,36]{0,1:T(8,128)S(1)} %slice.5), channel_id=1, source_target_pairs={{0,4},{1,5},{2,6},{3,7},{4,8},{5,9},{6,10},{7,11},{8,12},{9,13},{1... | collective-permute-start | bytes 10376
  644.9 3.4 convolution_convert_fusion
  649.0 0.7 copy.23
  (37 shorter events, 2.9 us)
Async XLA Ops:
  7.2 1.0 copy-start
  7.2 6.4 copy-start.8
  7.2 10.0 %copy-start.3 = (bf16[128,1152]{1,0:T(8,128)(2,1)S(1)}, bf16[128,1152]{1,0:T(8,128)(2,1)}, u32[]{:S(2)}) copy-start(bf16[128,1152]{1,0:T(8,128)(2,1)} %param.7) | copy-start | bytes 884740
  7.2 577.9 %all-reduce.5.cloned.1.call-start = ((), (), s32[]{:S(2)}) async-start(), calls=%async_computation | async-start | bytes 5308416
  11.7 39.3 %copy-start.2 = (bf16[128,1152]{0,1:T(8,128)(2,1)}, bf16[128,1152]{0,1:T(8,128)(2,1)S(1)}, u32[]{:S(2)}) copy-start(bf16[128,1152]{0,1:T(8,128)(2,1)S(1)} %bitcast_convert_fusion) | copy-start | bytes 884740
  11.7 23.9 %collective-permute-start.1 = (bf16[128,1152]{0,1:T(8,128)(2,1)S(1)}, bf16[128,1152]{0,1:T(8,128)(2,1)S(1)}, u32[]{:S(2)}, u32[]{:S(2)}) collective-permute-start(bf16[128,1152]{0,1:T(8,128)(2,1)S(1)} %bitcast_convert_fusion), channel_id=1, source_target_pairs={{752,0},{0,16},{16,32},{32,48},{48,64},{64,80},{80,96},{96,112},{1... | collective-permute-start | bytes 884744 | tf_op jit(solution)/shard_map/ppermute | solution.py:15
  13.6 22.0 %collective-permute-start = (s32[128]{0:T(128)S(1)}, s32[128]{0:T(128)S(1)}, u32[]{:S(2)}, u32[]{:S(2)}) collective-permute-start(s32[128]{0:T(128)S(1)} %copy-done.8), channel_id=1, source_target_pairs={{752,0},{0,16},{16,32},{32,48},{48,64},{64,80},{80,96},{96,112},{1... | collective-permute-start | bytes 1544 | tf_op jit(solution)/shard_map/ppermute | solution.py:15
  35.6 15.5 %copy-start.4 = (bf16[128,1152]{0,1:T(8,128)(2,1)}, bf16[128,1152]{0,1:T(8,128)(2,1)S(1)}, u32[]{:S(2)}) copy-start(bf16[128,1152]{0,1:T(8,128)(2,1)S(1)} %collective-permute-done.1) | copy-start | bytes 884740
  35.9 0.6 copy-start.7
  36.5 14.1 %collective-permute-start.2 = (f32[128,1152]{0,1:T(8,128)S(1)}, f32[128,1152]{0,1:T(8,128)S(1)}, u32[]{:S(2)}, u32[]{:S(2)}) collective-permute-start(f32[128,1152]{0,1:T(8,128)S(1)} %convolution_multiply_fusion), channel_id=1, source_target_pairs={{16,0},{32,16},{48,32},{64,48},{80,64},{96,80},{112,96},{128,112},... | collective-permute-start | bytes 1769480 | tf_op jit(solution)/shard_map/ppermute | solution.py:15
  38.8 14.4 %copy-start.6 = (bf16[128,128]{1,0:T(8,128)(2,1)}, bf16[128,128]{1,0:T(8,128)(2,1)S(1)}, u32[]{:S(2)}) copy-start(bf16[128,128]{1,0:T(8,128)(2,1)S(1)} %fusion.17) | copy-start | bytes 98308
  57.0 587.9 %copy-start.1 = (bf16[1152,1152]{1,0:T(8,128)(2,1)S(1)}, bf16[1152,1152]{1,0:T(8,128)(2,1)}, u32[]{:S(2)}) copy-start(bf16[1152,1152]{1,0:T(8,128)(2,1)} %param.11) | copy-start | bytes 7962628
  626.3 22.1 %copy-start.5 = (f32[24,48]{0,1:T(8,128)S(1)}, f32[24,48]{0,1:T(8,128)}, u32[]{:S(2)}) copy-start(f32[24,48]{0,1:T(8,128)} %fusion) | copy-start | bytes 13828
  626.3 22.1 %collective-permute-start.5 = (f32[24,48]{0,1:T(8,128)}, f32[24,48]{0,1:T(8,128)S(1)}, u32[]{:S(2)}, u32[]{:S(2)}) collective-permute-start(f32[24,48]{0,1:T(8,128)} %fusion), channel_id=1, source_target_pairs={{0,3},{1,4},{2,5},{3,6},{4,7},{5,8},{6,9},{7,10},{8,11},{9,12},{10... | collective-permute-start | bytes 13832
  631.8 16.5 %collective-permute-start.4 = (f32[24,48]{0,1:T(8,128)}, f32[24,48]{0,1:T(8,128)S(1)}, u32[]{:S(2)}, u32[]{:S(2)}) collective-permute-start(f32[24,48]{0,1:T(8,128)} %fusion), channel_id=1, source_target_pairs={{0,2},{1,3},{2,4},{3,5},{4,6},{5,7},{6,8},{7,9},{8,10},{9,11},{10,... | collective-permute-start | bytes 13832
  633.7 14.6 %collective-permute-start.3 = (f32[24,48]{0,1:T(8,128)}, f32[24,48]{0,1:T(8,128)S(1)}, u32[]{:S(2)}, u32[]{:S(2)}) collective-permute-start(f32[24,48]{0,1:T(8,128)} %fusion), channel_id=1, source_target_pairs={{0,1},{1,2},{2,3},{3,4},{4,5},{5,6},{6,7},{7,8},{8,9},{9,10},{10,1... | collective-permute-start | bytes 13832
  637.1 11.2 %collective-permute-start.6 = (f32[24,36]{0,1:T(8,128)S(1)}, f32[24,36]{0,1:T(8,128)S(1)}, u32[]{:S(2)}, u32[]{:S(2)}) collective-permute-start(f32[24,36]{0,1:T(8,128)S(1)} %slice.5), channel_id=1, source_target_pairs={{0,4},{1,5},{2,6},{3,7},{4,8},{5,9},{6,10},{7,11},{8,12},{9,13},{1... | collective-permute-start | bytes 10376
Sparse Core Ops, SparseCore 0:
  53.3 531.7 all-reduce.4
where the time goes:
time: 657 us
  waiting for transfers between devices  551 us (84%)
  blocking collectives  39.3 us (6%)
  starting transfers between devices  26 us (4%)
  between operations  16.9 us (3%)
  matrix products  12.7 us (2%)
  local copies, waits for them, and re-layouts  9.18 us (1%)
    unnamed x6, waiting for transfers between devices  523 us
    unnamed x1, blocking collectives  39.3 us
    ppermute x3, waiting for transfers between devices, shifted(): return lax.ppermute(block, axis, route)  28.5 us
    unnamed x5, starting transfers between devices  18.6 us
  transfers between devices with their start and end apart: 8, of which 3 were waited for; matrix products, arithmetic and copies ran while one was open for 2% of the time, Pallas kernels for 0%

commit v1 on v0

v1 whole, which is shorter than its diff:
```python
import functools

import jax
import jax.numpy as jnp
from jax import lax
from jax.experimental import pallas as pl
from jax.experimental.pallas import tpu as pltpu
from jax.sharding import PartitionSpec as P

D = 1152
HEAD_COLS = 576
ROWS = 128
EPSILON = 1e-06
MESH = pl.DeviceIdType.MESH
NX, NY, NZ, NC, ZL = 4, 8, 12, 2, 4
GROUP = NX * NC
W_CHUNKS = 3
WC = D // W_CHUNKS


def device_at(x, y, z, c):
    x, y, z, c = lax.rem(x, NX), lax.rem(y, NY), lax.rem(z, NZ), lax.rem(c, NC)
    return ((z // ZL) * NY + y) * NC + c, x * ZL + lax.rem(z, ZL)


def coefficients(logits, ids, base):
    image_rows = base + lax.broadcasted_iota(jnp.int32, logits.shape, 0)
    match = image_rows == ids
    value = jax.nn.sigmoid(jnp.where(match, -logits, logits))
    return jnp.where(match, -value, value).astype(jnp.bfloat16)


def nt(left, right):
    return lax.dot_general(left, right, (((1,), (1,)), ((), ())), preferred_element_type=jnp.float32)


def tn(left, right):
    return lax.dot_general(left, right, (((0,), (0,)), ((), ())), preferred_element_type=jnp.float32)


def unit_scale(values):
    return lax.rsqrt(jnp.sum(values * values, axis=1, keepdims=True) + EPSILON)


def kernel(
    img_hbm, desc_hbm, ids_hbm, w_hbm, dw_hbm, scale_ref, bias_ref,
    image_grad_hbm, text_grad_hbm, head_ref,
    imgs, img_units, descs, ids, ids_prev, w, dw, pert, proj, text_unit,
    at_send, at_all, pt_send, pt_all, r_buf, y_own, y_send, y_recv, z_send, z_recv,
    image_out, text_out,
    local_sem, out_sem, ring_send, ring_recv, a_send_sem, a_recv_sem, p_send_sem, p_recv_sem,
    y_send_sem, y_recv_sem, z_send_sem, z_recv_sem,
):
    b = lax.axis_index("blk")
    d = lax.axis_index("dp")
    c, y, z, x = lax.rem(b, 2), lax.rem(b // 2, NY), (b // (2 * NY)) * ZL + lax.rem(d, ZL), d // ZL
    after = (lax.rem(b + 1, 48), d)
    before = (lax.rem(b + 47, 48), d)
    group = [(i, f) for i in range(NX) for f in range(NC) if (i, f) != (0, 0)]

    barrier = pltpu.get_barrier_semaphore()
    for i, f in group:
        pl.semaphore_signal(barrier, inc=1, device_id=device_at(x + i, y, z, c + f), device_id_type=MESH)
    across = (lax.rem(b + 47 + 2 * c, 48), d)
    pl.semaphore_signal(barrier, inc=1, device_id=across, device_id_type=MESH)
    for j in range(1, NY):
        pl.semaphore_signal(barrier, inc=1, device_id=device_at(x, y + j, z, c), device_id_type=MESH)
    for j in range(1, NZ):
        pl.semaphore_signal(barrier, inc=1, device_id=device_at(x, y, z + j, c), device_id_type=MESH)

    loads = [
        pltpu.make_async_copy(desc_hbm, descs.at[pl.ds(0, ROWS)], local_sem.at[0]),
        pltpu.make_async_copy(img_hbm, imgs.at[pl.ds(0, ROWS)], local_sem.at[1]),
        pltpu.make_async_copy(ids_hbm, ids, local_sem.at[2]),
    ]
    loads[0].start()
    w_loads = []
    for n in range(W_CHUNKS):
        cols = pl.ds(n * WC, WC)
        pair = [
            pltpu.make_async_copy(w_hbm.at[:, cols], w.at[:, cols], local_sem.at[3 + 2 * n]),
            pltpu.make_async_copy(dw_hbm.at[:, cols], dw.at[:, cols], local_sem.at[4 + 2 * n]),
        ]
        for copy in pair:
            copy.start()
        w_loads.append(pair)
    loads[1].start()
    loads[2].start()

    loads[0].wait()
    desc = descs[pl.ds(0, ROWS), :]
    turned = jnp.transpose(desc.astype(jnp.float32)).reshape(24, 2, 24, ROWS)
    for parity in range(2):
        at_send[parity] = turned[:, parity].reshape(HEAD_COLS, ROWS).astype(jnp.bfloat16)
    loads[1].wait()
    loads[2].wait()

    pl.semaphore_wait(barrier, len(group) + 1 + NY - 1 + NZ - 1)

    def remote(src, dst, send, recv, device):
        return pltpu.make_async_remote_copy(
            src_ref=src, dst_ref=dst, send_sem=send, recv_sem=recv, device_id=device, device_id_type=MESH
        )

    send_img = remote(imgs.at[pl.ds(0, ROWS)], imgs.at[pl.ds(ROWS, ROWS)], ring_send.at[0], ring_recv.at[0], before)
    send_img.start()
    send_desc = remote(descs.at[pl.ds(0, ROWS)], descs.at[pl.ds(ROWS, ROWS)], ring_send.at[1], ring_recv.at[1], after)
    send_ids = remote(ids, ids_prev, ring_send.at[2], ring_recv.at[2], after)
    a_copies = []
    for i, f in group:
        s = i * NC + f
        copy = remote(
            at_send.at[lax.rem(c + f, NC)], at_all.at[:, pl.ds(s * ROWS, ROWS)],
            a_send_sem.at[s], a_recv_sem.at[s], device_at(x + i, y, z, c + f),
        )
        copy.start()
        a_copies.append(copy)
    send_desc.start()
    send_ids.start()

    for n in range(W_CHUNKS):
        cols = pl.ds(n * WC, WC)
        for copy in w_loads[n]:
            copy.wait()
        part = (w[:, cols].astype(jnp.float32) + dw[:, cols].astype(jnp.float32)).astype(jnp.bfloat16)
        pert[:, cols] = part
        proj[:, cols] = jnp.dot(descs[pl.ds(0, ROWS), :], part, preferred_element_type=jnp.float32)
    projected = proj[...]
    text_scale = unit_scale(projected)
    unit = projected * text_scale
    proj[...] = unit
    text_unit[pl.ds(0, ROWS), :] = unit.astype(jnp.bfloat16)

    img = imgs[pl.ds(0, ROWS), :].astype(jnp.float32)
    image_scale = unit_scale(img)
    img_units[pl.ds(0, ROWS), :] = (img * image_scale).astype(jnp.bfloat16)
    at_all[:, pl.ds(0, ROWS)] = at_send[c]

    scale = scale_ref[0]
    bias = bias_ref[0]
    row_base = (b * 16 + d) * ROWS
    next_base = (after[0] * 16 + d) * ROWS

    send_img.wait_recv()
    img_next = imgs[pl.ds(ROWS, ROWS), :].astype(jnp.float32)
    img_units[pl.ds(ROWS, ROWS), :] = (img_next * unit_scale(img_next)).astype(jnp.bfloat16)
    logits = scale * nt(img_units[...], text_unit[pl.ds(0, ROWS), :]) + bias
    my_ids = ids[...]
    coef_own = coefficients(logits[:ROWS], my_ids, row_base)
    coef_next = coefficients(logits[ROWS:], my_ids, next_base)
    unit_text_grad = scale * tn(jnp.concatenate([coef_own, coef_next], axis=0), img_units[...])
    along = jnp.sum(unit * unit_text_grad, axis=1, keepdims=True)
    pre_grad = text_scale * (unit_text_grad - unit * along)
    pt = jnp.transpose(pre_grad[:, :HEAD_COLS])
    pt_send[...] = pt.reshape(NX, HEAD_COLS // NX, ROWS).astype(jnp.bfloat16)
    p_copies = []
    for i, f in group:
        s = i * NC + f
        copy = remote(
            pt_send.at[lax.rem(x + i, NX)], pt_all.at[:, pl.ds(s * ROWS, ROWS)],
            p_send_sem.at[s], p_recv_sem.at[s], device_at(x + i, y, z, c + f),
        )
        copy.start()
        p_copies.append(copy)
    pt_all[:, pl.ds(0, ROWS)] = pt_send[x]

    text_out[...] = nt(pre_grad.astype(jnp.bfloat16), pert[...]).astype(jnp.bfloat16)
    text_copy = pltpu.make_async_copy(text_out, text_grad_hbm, out_sem.at[0])
    text_copy.start()

    for copy in a_copies:
        copy.wait_recv()
    for copy in p_copies:
        copy.wait_recv()
    r_buf[:, pl.ds(0, 144)] = nt(at_all[...], pt_all[...])
    low = r_buf[:, pl.ds(0, 128)].reshape(24, 3, 8, 128)
    high = r_buf[:, pl.ds(128, 128)].reshape(24, 3, 8, 128)
    lane = lax.broadcasted_iota(jnp.int32, (24, 8, 128), 2)

    def moved(values, shift):
        shift = shift % 128
        return pltpu.roll(values, shift, 2) if shift else values

    for k in range(ZL):
        parts = []
        for o in range(3):
            part = moved(low[:, o], 36 * o - 36 * k)
            if k == ZL - 1:
                part = jnp.where(lane < 36 * o + 20, part, moved(high[:, o], 36 * o + 20))
            parts.append(part)
        tile = jnp.where(lane < 36, parts[0], jnp.where(lane < 72, parts[1], parts[2]))
        tile = jnp.where(lane < 108, tile, 0.0).reshape(3, NY, 8, 128)
        for h in range(3):
            y_own[:, pl.ds((h * ZL + k) * 8, 8), :] = tile[h]
    y_send[...] = y_own[...].astype(jnp.bfloat16)
    y_copies = []
    for j in range(1, NY):
        copy = remote(
            y_send.at[lax.rem(y + j, NY)], y_recv.at[j], y_send_sem.at[j], y_recv_sem.at[j], device_at(x, y + j, z, c)
        )
        copy.start()
        y_copies.append(copy)

    send_desc.wait_recv()
    send_ids.wait_recv()
    projected_prev = jnp.dot(descs[pl.ds(ROWS, ROWS), :], pert[...], preferred_element_type=jnp.float32)
    text_unit[pl.ds(ROWS, ROWS), :] = (projected_prev * unit_scale(projected_prev)).astype(jnp.bfloat16)
    logits_prev = scale * nt(img_units[pl.ds(0, ROWS), :], text_unit[pl.ds(ROWS, ROWS), :]) + bias
    coef_prev = coefficients(logits_prev, ids_prev[...], row_base)
    unit_image_grad = scale * jnp.dot(
        jnp.concatenate([coef_own, coef_prev], axis=1), text_unit[...], preferred_element_type=jnp.float32
    )
    img = imgs[pl.ds(0, ROWS), :].astype(jnp.float32)
    image_dir = img * image_scale
    along_image = jnp.sum(image_dir * unit_image_grad, axis=1, keepdims=True)
    image_out[...] = (image_scale * (unit_image_grad - image_dir * along_image)).astype(jnp.bfloat16)
    image_copy = pltpu.make_async_copy(image_out, image_grad_hbm, out_sem.at[1])
    image_copy.start()

    total = y_own[y]
    for j, copy in zip(range(1, NY), y_copies):
        copy.wait_recv()
        total = total + y_recv[j].astype(jnp.float32)
    z_send[...] = total.reshape(NZ, 8, 128)
    z_copies = []
    for j in range(1, NZ):
        copy = remote(
            z_send.at[lax.rem(z + j, NZ)], z_recv.at[j], z_send_sem.at[j], z_recv_sem.at[j], device_at(x, y, z + j, c)
        )
        copy.start()
        z_copies.append(copy)
    block = z_send[z]
    for j, copy in zip(range(1, NZ), z_copies):
        copy.wait_recv()
        block = block + z_recv[j]
    for o in range(3):
        head_ref[pl.ds(8 * o, 8), :] = (pltpu.roll(block, 128 - 36 * o, 1) if o else block)[:, :36]

    for copy in [send_img, send_desc, send_ids, *a_copies, *p_copies, *y_copies, *z_copies]:
        copy.wait_send()
    text_copy.wait()
    image_copy.wait()


def shards(img, desc, ids, w, dw, scale, bias):
    bf16, f32 = jnp.bfloat16, jnp.float32
    any_spec = pl.BlockSpec(memory_space=pl.ANY)
    smem = pl.BlockSpec(memory_space=pltpu.SMEM)
    dma = pltpu.SemaphoreType.DMA
    return pl.pallas_call(
        kernel,
        out_shape=(
            jax.ShapeDtypeStruct((ROWS, D), bf16),
            jax.ShapeDtypeStruct((ROWS, D), bf16),
            jax.ShapeDtypeStruct((24, 36), f32),
        ),
        in_specs=[any_spec] * 5 + [smem] * 2,
        out_specs=(any_spec, any_spec, pl.BlockSpec(memory_space=pltpu.VMEM)),
        scratch_shapes=[
            pltpu.VMEM((2 * ROWS, D), bf16),
            pltpu.VMEM((2 * ROWS, D), bf16),
            pltpu.VMEM((2 * ROWS, D), bf16),
            pltpu.VMEM((1, ROWS), jnp.int32),
            pltpu.VMEM((1, ROWS), jnp.int32),
            pltpu.VMEM((D, D), bf16),
            pltpu.VMEM((D, D), bf16),
            pltpu.VMEM((D, D), bf16),
            pltpu.VMEM((ROWS, D), f32),
            pltpu.VMEM((2 * ROWS, D), bf16),
            pltpu.VMEM((2, HEAD_COLS, ROWS), bf16),
            pltpu.VMEM((HEAD_COLS, GROUP * ROWS), bf16),
            pltpu.VMEM((NX, HEAD_COLS // NX, ROWS), bf16),
            pltpu.VMEM((HEAD_COLS // NX, GROUP * ROWS), bf16),
            pltpu.VMEM((HEAD_COLS, 256), f32),
            pltpu.VMEM((NY, 96, 128), f32),
            pltpu.VMEM((NY, 96, 128), bf16),
            pltpu.VMEM((NY, 96, 128), bf16),
            pltpu.VMEM((NZ, 8, 128), f32),
            pltpu.VMEM((NZ, 8, 128), f32),
            pltpu.VMEM((ROWS, D), bf16),
            pltpu.VMEM((ROWS, D), bf16),
            dma((3 + 2 * W_CHUNKS,)),
            dma((2,)),
            dma((3,)),
            dma((3,)),
            dma((GROUP,)),
            dma((GROUP,)),
            dma((GROUP,)),
            dma((GROUP,)),
            dma((NY,)),
            dma((NY,)),
            dma((NZ,)),
            dma((NZ,)),
        ],
        compiler_params=pltpu.CompilerParams(
            collective_id=0, has_side_effects=True, vmem_limit_bytes=63 << 20
        ),
        name="contrastive",
    )(img, desc, ids.reshape(1, ROWS), w, dw, scale.reshape(1), bias.reshape(1))


def solution(mesh):
    rows = P(("blk", "dp"), None)
    return jax.shard_map(
        shards,
        mesh=mesh,
        in_specs=(rows, rows, P(("blk", "dp")), P(), P(), P(), P()),
        out_specs=(rows, rows, P("blk", "dp")),
        check_vma=False,
    )
```

time: 657 us -> 60.9 us (0.09)
  the two profiles are of different devices: /device:TPU:66 before, /device:TPU:16 now
where the time goes in v1:
time: 60.9 us; the launch traced here: 60.6 us
  Pallas kernels  54 us (89%)
  local copies, waits for them, and re-layouts  4.7 us (8%)
  between operations  1.93 us (3%)
    pallas_call x1, Pallas kernels, shards(): pl.pallas_call(kernel, out_shape=(jax.ShapeDtypeStruct((ROWS, D), bf16),...  54 us
    unnamed x3, local copies, waits for them, and re-layouts  4.7 us

profile of v1, /device:TPU:16, one launch (start us, length us, event | category | flops | bytes accessed | tf_op | source)
XLA Modules:
  0.0 60.6 jit_solution(12708443843519452343)
XLA Ops:
  1.9 54.0 %contrastive.1 = (bf16[128,1152]{1,0:T(8,128)(2,1)}, bf16[128,1152]{1,0:T(8,128)(2,1)}, f32[24,36]{1,0:T(8,128)}) custom-call(bf16[128,1152]{1,0:T(8,128)(2,1)} %img_hbm.1, bf16[128,1152]{1,0:T(8,128)(2,1)} %desc_hbm.1, s32[1,128]{1,0:T(1,128)} %bitcast.5, bf16[1152,1152]{1,0:T(8,128)(2,1)} %w_hbm.1, bf16[1152,1152]{1,0:T(8,128)(2,1)} %dw_hbm.1, ...), custom_call_target="tpu_custom_call" | custom-call | tf_op jit(solution)/shard_map/contrastive/pallas_call | solution.py:250
  55.9 1.7 %copy.15 = bf16[128,1152]{1,0:T(8,128)(2,1)} copy(bf16[128,1152]{1,0:T(8,128)(2,1)} %get-tuple-element.6) | data formatting | bytes 589824
  57.6 1.7 %copy.16 = bf16[128,1152]{1,0:T(8,128)(2,1)} copy(bf16[128,1152]{1,0:T(8,128)(2,1)} %get-tuple-element.7) | data formatting | bytes 589824
  59.3 1.3 %copy.17 = f32[24,36]{1,0:T(8,128)} copy(f32[24,36]{1,0:T(8,128)} %get-tuple-element.8) | data formatting | bytes 6912

commit v2 on v1

--- a/solution.py
+++ b/solution.py
@@ -15,6 +15,10 @@
 NX, NY, NZ, NC, ZL = 4, 8, 12, 2, 4
 GROUP = NX * NC
 W_CHUNKS = 3
+PLACE_PARTS = 4
+IMG_PARTS = ((0, 64), (64, 32), (96, 32))
+Y_ORDER = (4, 3, 5, 2, 6, 1, 7)
+Z_ORDER = (6, 5, 7, 4, 8, 3, 9, 2, 10, 1, 11)
 WC = D // W_CHUNKS
 
 
@@ -49,7 +53,7 @@
     at_send, at_all, pt_send, pt_all, r_buf, y_own, y_send, y_recv, z_send, z_recv,
     image_out, text_out,
     local_sem, out_sem, ring_send, ring_recv, a_send_sem, a_recv_sem, p_send_sem, p_recv_sem,
-    y_send_sem, y_recv_sem, z_send_sem, z_recv_sem,
+    y_send_sem, y_recv_sem, z_send_sem, z_recv_sem, word, ready, carried, help_recv, carry_send,
 ):
     b = lax.axis_index("blk")
     d = lax.axis_index("dp")
@@ -62,10 +66,23 @@
     for i, f in group:
         pl.semaphore_signal(barrier, inc=1, device_id=device_at(x + i, y, z, c + f), device_id_type=MESH)
     across = (lax.rem(b + 47 + 2 * c, 48), d)
-    pl.semaphore_signal(barrier, inc=1, device_id=across, device_id_type=MESH)
-    for j in range(1, NY):
+    goes_out = jnp.logical_and(y == 0, c == 0)
+    comes_in = jnp.logical_and(y == NY - 1, c == 1)
+    helps = jnp.logical_and(jnp.logical_or(y == NY - 1, y == 1), c == 0)
+    helpers = [device_at(x, NY - 1, z + ZL, 0), device_at(x, 1, z + ZL, 0)]
+
+    @pl.when(jnp.logical_not(goes_out))
+    def _():
+        pl.semaphore_signal(barrier, inc=1, device_id=across, device_id_type=MESH)
+
+    @pl.when(comes_in)
+    def _():
+        for helper in helpers:
+            pl.semaphore_signal(barrier, inc=1, device_id=helper, device_id_type=MESH)
+
+    for j in (1, NY - 1):
         pl.semaphore_signal(barrier, inc=1, device_id=device_at(x, y + j, z, c), device_id_type=MESH)
-    for j in range(1, NZ):
+    for j in (1, NZ - 1):
         pl.semaphore_signal(barrier, inc=1, device_id=device_at(x, y, z + j, c), device_id_type=MESH)
 
     loads = [
@@ -73,7 +90,8 @@
         pltpu.make_async_copy(img_hbm, imgs.at[pl.ds(0, ROWS)], local_sem.at[1]),
         pltpu.make_async_copy(ids_hbm, ids, local_sem.at[2]),
     ]
-    loads[0].start()
+    for copy in loads:
+        copy.start()
     w_loads = []
     for n in range(W_CHUNKS):
         cols = pl.ds(n * WC, WC)
@@ -84,39 +102,76 @@
         for copy in pair:
             copy.start()
         w_loads.append(pair)
-    loads[1].start()
-    loads[2].start()
 
     loads[0].wait()
     desc = descs[pl.ds(0, ROWS), :]
     turned = jnp.transpose(desc.astype(jnp.float32)).reshape(24, 2, 24, ROWS)
     for parity in range(2):
         at_send[parity] = turned[:, parity].reshape(HEAD_COLS, ROWS).astype(jnp.bfloat16)
-    loads[1].wait()
-    loads[2].wait()
-
-    pl.semaphore_wait(barrier, len(group) + 1 + NY - 1 + NZ - 1)
+    for copy in loads[1:]:
+        copy.wait()
+
+    pl.semaphore_wait(barrier, len(group) + 4 + jnp.where(comes_in, 0, 1) + jnp.where(helps, 1, 0))
+
+    def pass_on(round_, along_y, along_z):
+        for j in along_y:
+            pl.semaphore_signal(
+                word.at[2 * round_], inc=1, device_id=device_at(x, y + j, z, c), device_id_type=MESH
+            )
+        for j in along_z:
+            pl.semaphore_signal(
+                word.at[2 * round_ + 1], inc=1, device_id=device_at(x, y, z + j, c), device_id_type=MESH
+            )
+
+    pass_on(0, (1, NY - 1), (1, NZ - 1))
 
     def remote(src, dst, send, recv, device):
         return pltpu.make_async_remote_copy(
             src_ref=src, dst_ref=dst, send_sem=send, recv_sem=recv, device_id=device, device_id_type=MESH
         )
 
-    send_img = remote(imgs.at[pl.ds(0, ROWS)], imgs.at[pl.ds(ROWS, ROWS)], ring_send.at[0], ring_recv.at[0], before)
-    send_img.start()
-    send_desc = remote(descs.at[pl.ds(0, ROWS)], descs.at[pl.ds(ROWS, ROWS)], ring_send.at[1], ring_recv.at[1], after)
-    send_ids = remote(ids, ids_prev, ring_send.at[2], ring_recv.at[2], after)
+    def img_part(part, device):
+        rows, n = IMG_PARTS[part]
+        return remote(
+            imgs.at[pl.ds(rows, n)], imgs.at[pl.ds(ROWS + rows, n)], ring_send.at[part], ring_recv.at[part], device
+        )
+
+    def help_part(part, device):
+        rows, n = IMG_PARTS[part]
+        return remote(imgs.at[pl.ds(rows, n)], carried, ring_send.at[part], help_recv, device)
+
+    send_img = [img_part(part, before) for part in range(3)]
+
+    @pl.when(goes_out)
+    def _():
+        pl.semaphore_signal(ready, inc=1, device_id=across, device_id_type=MESH)
+        help_part(1, device_at(x, NY - 1, z, 0)).start()
+        help_part(2, device_at(x, 1, z, 0)).start()
+        send_img[0].start()
+
+    @pl.when(jnp.logical_not(goes_out))
+    def _():
+        for copy in send_img:
+            copy.start()
+
+    def slot(i, core):
+        return i * NC + core
+
+    first = jnp.where(c == 0, NX - 1, 1)
     a_copies = []
-    for i, f in group:
-        s = i * NC + f
+    for n, (i, f) in enumerate([(first, 0), (first, 1), (0, 1), (NX - first, 0), (NX - first, 1)]):
         copy = remote(
-            at_send.at[lax.rem(c + f, NC)], at_all.at[:, pl.ds(s * ROWS, ROWS)],
-            a_send_sem.at[s], a_recv_sem.at[s], device_at(x + i, y, z, c + f),
+            at_send.at[lax.rem(c + f, NC)], at_all.at[slot(i, c)],
+            a_send_sem.at[n], a_recv_sem.at[slot(i, c)], device_at(x + i, y, z, c + f),
         )
         copy.start()
         a_copies.append(copy)
-    send_desc.start()
-    send_ids.start()
+
+    def a_arrived(s):
+        return remote(at_send.at[0], at_all.at[s], a_send_sem.at[0], a_recv_sem.at[s], before)
+
+    def p_arrived(s):
+        return remote(pt_send.at[0], pt_all.at[s], p_send_sem.at[0], p_recv_sem.at[s], before)
 
     for n in range(W_CHUNKS):
         cols = pl.ds(n * WC, WC)
@@ -125,6 +180,10 @@
         part = (w[:, cols].astype(jnp.float32) + dw[:, cols].astype(jnp.float32)).astype(jnp.bfloat16)
         pert[:, cols] = part
         proj[:, cols] = jnp.dot(descs[pl.ds(0, ROWS), :], part, preferred_element_type=jnp.float32)
+    pl.semaphore_wait(word.at[0], 2)
+    pl.semaphore_wait(word.at[1], 2)
+    pass_on(1, (2, NY - 2), (2, NZ - 2))
+
     projected = proj[...]
     text_scale = unit_scale(projected)
     unit = projected * text_scale
@@ -134,14 +193,45 @@
     img = imgs[pl.ds(0, ROWS), :].astype(jnp.float32)
     image_scale = unit_scale(img)
     img_units[pl.ds(0, ROWS), :] = (img * image_scale).astype(jnp.bfloat16)
-    at_all[:, pl.ds(0, ROWS)] = at_send[c]
-
-    scale = scale_ref[0]
-    bias = bias_ref[0]
+    at_all[slot(0, c)] = at_send[c]
+
+    carry = remote(
+        carried,
+        imgs.at[pl.ds(ROWS + IMG_PARTS[1][0] + jnp.where(y == 1, IMG_PARTS[1][1], 0), IMG_PARTS[1][1])],
+        carry_send, ring_recv.at[jnp.where(y == 1, 2, 1)], device_at(x, NY - 1, z + NZ - ZL, 1),
+    )
+
+    @pl.when(helps)
+    def _():
+        help_part(1, before).wait_recv()
+        carry.start()
+
+    @pl.when(comes_in)
+    def _():
+        pl.semaphore_wait(ready, 1)
+
+    send_desc = remote(descs.at[pl.ds(0, ROWS)], descs.at[pl.ds(ROWS, ROWS)], ring_send.at[3], ring_recv.at[3], after)
+    send_ids = remote(ids, ids_prev, ring_send.at[4], ring_recv.at[4], after)
+    send_desc.start()
+    send_ids.start()
+
+    handed = []
+    for n, (i, core) in enumerate([(NX - 1, 0), (1, 1)]):
+        a_arrived(slot(i, core)).wait_recv()
+        copy = remote(
+            at_all.at[slot(i, core)], at_all.at[slot(2, core)],
+            a_send_sem.at[5 + n], a_recv_sem.at[slot(2, core)], device_at(x + i, y, z, c),
+        )
+        copy.start()
+        handed.append(copy)
+
+    scale = scale_ref[...]
+    bias = bias_ref[...]
     row_base = (b * 16 + d) * ROWS
     next_base = (after[0] * 16 + d) * ROWS
 
-    send_img.wait_recv()
+    for copy in send_img:
+        copy.wait_recv()
     img_next = imgs[pl.ds(ROWS, ROWS), :].astype(jnp.float32)
     img_units[pl.ds(ROWS, ROWS), :] = (img_next * unit_scale(img_next)).astype(jnp.bfloat16)
     logits = scale * nt(img_units[...], text_unit[pl.ds(0, ROWS), :]) + bias
@@ -154,25 +244,34 @@
     pt = jnp.transpose(pre_grad[:, :HEAD_COLS])
     pt_send[...] = pt.reshape(NX, HEAD_COLS // NX, ROWS).astype(jnp.bfloat16)
     p_copies = []
-    for i, f in group:
-        s = i * NC + f
+    for n, (i, f) in enumerate([(2, 0), (2, 1), (1, 0), (1, 1), (3, 0), (3, 1), (0, 1)]):
         copy = remote(
-            pt_send.at[lax.rem(x + i, NX)], pt_all.at[:, pl.ds(s * ROWS, ROWS)],
-            p_send_sem.at[s], p_recv_sem.at[s], device_at(x + i, y, z, c + f),
+            pt_send.at[lax.rem(x + i, NX)], pt_all.at[slot(i, c)],
+            p_send_sem.at[n], p_recv_sem.at[slot(i, c)], device_at(x + i, y, z, c + f),
         )
         copy.start()
         p_copies.append(copy)
-    pt_all[:, pl.ds(0, ROWS)] = pt_send[x]
+    pt_all[slot(0, c)] = pt_send[x]
+
+    pl.semaphore_wait(word.at[2], 2)
+    pl.semaphore_wait(word.at[3], 2)
+    pass_on(2, (), (2, NZ - 2))
 
     text_out[...] = nt(pre_grad.astype(jnp.bfloat16), pert[...]).astype(jnp.bfloat16)
     text_copy = pltpu.make_async_copy(text_out, text_grad_hbm, out_sem.at[0])
     text_copy.start()
 
-    for copy in a_copies:
-        copy.wait_recv()
-    for copy in p_copies:
-        copy.wait_recv()
-    r_buf[:, pl.ds(0, 144)] = nt(at_all[...], pt_all[...])
+    for i in range(NX):
+        for core in range(NC):
+            if i in (1, 2, 3) and (i, core) not in ((NX - 1, 0), (1, 1)):
+                a_arrived(slot(i, core)).wait_recv()
+            if i:
+                p_arrived(slot(i, core)).wait_recv()
+    a_arrived(slot(0, 1 - c)).wait_recv()
+    p_arrived(slot(0, 1 - c)).wait_recv()
+    features = jnp.concatenate([at_all[s] for s in range(GROUP)], axis=1)
+    columns = jnp.concatenate([pt_all[s] for s in range(GROUP)], axis=1)
+    r_buf[:, pl.ds(0, 144)] = nt(features, columns)
     low = r_buf[:, pl.ds(0, 128)].reshape(24, 3, 8, 128)
     high = r_buf[:, pl.ds(128, 128)].reshape(24, 3, 8, 128)
     lane = lax.broadcasted_iota(jnp.int32, (24, 8, 128), 2)
@@ -194,13 +293,26 @@
             y_own[:, pl.ds((h * ZL + k) * 8, 8), :] = tile[h]
     y_send[...] = y_own[...].astype(jnp.bfloat16)
     y_copies = []
-    for j in range(1, NY):
+    for j in Y_ORDER:
         copy = remote(
             y_send.at[lax.rem(y + j, NY)], y_recv.at[j], y_send_sem.at[j], y_recv_sem.at[j], device_at(x, y + j, z, c)
         )
         copy.start()
         y_copies.append(copy)
 
+    total = y_own[y]
+    for j, copy in sorted(zip(Y_ORDER, y_copies), key=lambda e: min(e[0], NY - e[0])):
+        copy.wait_recv()
+        total = total + y_recv[j].astype(jnp.float32)
+    pl.semaphore_wait(word.at[5], 2)
+    z_send[...] = total.reshape(NZ, 8, 128)
+    z_copies = []
+    for j in Z_ORDER:
+        copy = remote(
+            z_send.at[lax.rem(z + j, NZ)], z_recv.at[j], z_send_sem.at[j], z_recv_sem.at[j], device_at(x, y, z + j, c)
+        )
+        copy.start()
+        z_copies.append(copy)
     send_desc.wait_recv()
     send_ids.wait_recv()
     projected_prev = jnp.dot(descs[pl.ds(ROWS, ROWS), :], pert[...], preferred_element_type=jnp.float32)
@@ -217,44 +329,54 @@
     image_copy = pltpu.make_async_copy(image_out, image_grad_hbm, out_sem.at[1])
     image_copy.start()
 
-    total = y_own[y]
-    for j, copy in zip(range(1, NY), y_copies):
-        copy.wait_recv()
-        total = total + y_recv[j].astype(jnp.float32)
-    z_send[...] = total.reshape(NZ, 8, 128)
-    z_copies = []
-    for j in range(1, NZ):
-        copy = remote(
-            z_send.at[lax.rem(z + j, NZ)], z_recv.at[j], z_send_sem.at[j], z_recv_sem.at[j], device_at(x, y, z + j, c)
-        )
-        copy.start()
-        z_copies.append(copy)
     block = z_send[z]
-    for j, copy in zip(range(1, NZ), z_copies):
+    for j, copy in sorted(zip(Z_ORDER, z_copies), key=lambda e: min(e[0], NZ - e[0])):
         copy.wait_recv()
         block = block + z_recv[j]
     for o in range(3):
         head_ref[pl.ds(8 * o, 8), :] = (pltpu.roll(block, 128 - 36 * o, 1) if o else block)[:, :36]
 
-    for copy in [send_img, send_desc, send_ids, *a_copies, *p_copies, *y_copies, *z_copies]:
+    for copy in [*send_img, send_desc, send_ids, *a_copies, *handed, *p_copies, *y_copies, *z_copies]:
         copy.wait_send()
+
+    @pl.when(helps)
+    def _():
+        carry.wait_send()
+
     text_copy.wait()
     image_copy.wait()
+
+
+def placed(image_in, text_in, head_in, image_out, text_out, head_out, image, text, head, sem):
+    pairs = [(head_in, head, head_out)]
+    step = ROWS // PLACE_PARTS
+    for n in range(PLACE_PARTS):
+        rows = pl.ds(n * step, step)
+        pairs.append((image_in.at[rows], image.at[rows], image_out.at[rows]))
+        pairs.append((text_in.at[rows], text.at[rows], text_out.at[rows]))
+    reads = [pltpu.make_async_copy(a, b, sem.at[0, n]) for n, (a, b, _) in enumerate(pairs)]
+    writes = [pltpu.make_async_copy(b, c, sem.at[1, n]) for n, (_, b, c) in enumerate(pairs)]
+    for copy in reads:
+        copy.start()
+    for read, write in zip(reads, writes):
+        read.wait()
+        write.start()
+    for copy in writes:
+        copy.wait()
 
 
 def shards(img, desc, ids, w, dw, scale, bias):
     bf16, f32 = jnp.bfloat16, jnp.float32
     any_spec = pl.BlockSpec(memory_space=pl.ANY)
-    smem = pl.BlockSpec(memory_space=pltpu.SMEM)
     dma = pltpu.SemaphoreType.DMA
-    return pl.pallas_call(
+    results = pl.pallas_call(
         kernel,
         out_shape=(
             jax.ShapeDtypeStruct((ROWS, D), bf16),
             jax.ShapeDtypeStruct((ROWS, D), bf16),
             jax.ShapeDtypeStruct((24, 36), f32),
         ),
-        in_specs=[any_spec] * 5 + [smem] * 2,
+        in_specs=[any_spec] * 5 + [pl.BlockSpec(memory_space=pltpu.SMEM)] * 2,
         out_specs=(any_spec, any_spec, pl.BlockSpec(memory_space=pltpu.VMEM)),
         scratch_shapes=[
             pltpu.VMEM((2 * ROWS, D), bf16),
@@ -268,9 +390,9 @@
             pltpu.VMEM((ROWS, D), f32),
             pltpu.VMEM((2 * ROWS, D), bf16),
             pltpu.VMEM((2, HEAD_COLS, ROWS), bf16),
-            pltpu.VMEM((HEAD_COLS, GROUP * ROWS), bf16),
+            pltpu.VMEM((GROUP, HEAD_COLS, ROWS), bf16),
             pltpu.VMEM((NX, HEAD_COLS // NX, ROWS), bf16),
-            pltpu.VMEM((HEAD_COLS // NX, GROUP * ROWS), bf16),
+            pltpu.VMEM((GROUP, HEAD_COLS // NX, ROWS), bf16),
             pltpu.VMEM((HEAD_COLS, 256), f32),
             pltpu.VMEM((NY, 96, 128), f32),
             pltpu.VMEM((NY, 96, 128), bf16),
@@ -279,10 +401,10 @@
             pltpu.VMEM((NZ, 8, 128), f32),
             pltpu.VMEM((ROWS, D), bf16),
             pltpu.VMEM((ROWS, D), bf16),
-            dma((3 + 2 * W_CHUNKS,)),
+            dma((4 + 2 * W_CHUNKS,)),
             dma((2,)),
-            dma((3,)),
-            dma((3,)),
+            dma((5,)),
+            dma((5,)),
             dma((GROUP,)),
             dma((GROUP,)),
             dma((GROUP,)),
@@ -291,12 +413,29 @@
             dma((NY,)),
             dma((NZ,)),
             dma((NZ,)),
+            pltpu.SemaphoreType.REGULAR((6,)),
+            pltpu.SemaphoreType.REGULAR,
+            pltpu.VMEM((IMG_PARTS[1][1], D), bf16),
+            dma,
+            dma,
         ],
         compiler_params=pltpu.CompilerParams(
             collective_id=0, has_side_effects=True, vmem_limit_bytes=63 << 20
         ),
         name="contrastive",
-    )(img, desc, ids.reshape(1, ROWS), w, dw, scale.reshape(1), bias.reshape(1))
+    )(img, desc, ids.reshape(1, ROWS), w, dw, scale, bias)
+    return pl.pallas_call(
+        placed,
+        out_shape=[jax.ShapeDtypeStruct(r.shape, r.dtype) for r in results],
+        in_specs=[any_spec] * 3,
+        out_specs=[any_spec] * 3,
+        scratch_shapes=[
+            *[pltpu.VMEM(r.shape, r.dtype) for r in results],
+            dma((2, 2 * PLACE_PARTS + 1)),
+        ],
+        compiler_params=pltpu.CompilerParams(vmem_limit_bytes=63 << 20),
+        name="placed",
+    )(*results)
 
 
 def solution(mesh):

time: 60.9 us -> 51 us (0.84)
  the two profiles are of different devices: /device:TPU:16 before, /device:TPU:1 now
where the time goes in v2:
time: 51 us; the launch traced here: 50.8 us
  Pallas kernels  48.8 us (96%)
  between operations  1.93 us (4%)
    pallas_call x1, Pallas kernels, shards(): pl.pallas_call(kernel, out_shape=(jax.ShapeDtypeStruct((ROWS, D), bf16),...  46.9 us
    pallas_call x1, Pallas kernels, shards(): pl.pallas_call(placed, out_shape=[jax.ShapeDtypeStruct(r.shape, r.dtype)...  1.94 us

profile of v2, /device:TPU:1, one launch (start us, length us, event | category | flops | bytes accessed | tf_op | source)
XLA Modules:
  0.0 50.8 jit_solution(17611326976621977811)
XLA Ops:
  1.9 46.9 %contrastive.1 = (bf16[128,1152]{1,0:T(8,128)(2,1)}, bf16[128,1152]{1,0:T(8,128)(2,1)}, f32[24,36]{1,0:T(8,128)}) custom-call(bf16[128,1152]{1,0:T(8,128)(2,1)} %img_hbm.1, bf16[128,1152]{1,0:T(8,128)(2,1)} %desc_hbm.1, s32[1,128]{1,0:T(1,128)} %bitcast.1, bf16[1152,1152]{1,0:T(8,128)(2,1)} %w_hbm.1, bf16[1152,1152]{1,0:T(8,128)(2,1)} %dw_hbm.1, ...), custom_call_target="tpu_custom_call" | custom-call | tf_op jit(solution)/shard_map/contrastive/pallas_call | solution.py:372
  48.8 1.9 %placed.1 = (bf16[128,1152]{1,0:T(8,128)(2,1)}, bf16[128,1152]{1,0:T(8,128)(2,1)}, f32[24,36]{1,0:T(8,128)}) custom-call(bf16[128,1152]{1,0:T(8,128)(2,1)} %get-tuple-element.6.image_in, bf16[128,1152]{1,0:T(8,128)(2,1)} %get-tuple-element.7.text_in, f32[24,36]{1,0:T(8,128)} %get-tuple-element.8.head_in), custom_call_target="tpu_custom_call" | custom-call | tf_op jit(solution)/shard_map/placed/pallas_call | solution.py:427

commit v3 on v2

--- a/solution.py
+++ b/solution.py
@@ -48,11 +48,10 @@
 
 def kernel(
     img_hbm, desc_hbm, ids_hbm, w_hbm, dw_hbm, scale_ref, bias_ref,
-    image_grad_hbm, text_grad_hbm, head_ref,
+    image_out, text_out, head_ref,
     imgs, img_units, descs, ids, ids_prev, w, dw, pert, proj, text_unit,
     at_send, at_all, pt_send, pt_all, r_buf, y_own, y_send, y_recv, z_send, z_recv,
-    image_out, text_out,
-    local_sem, out_sem, ring_send, ring_recv, a_send_sem, a_recv_sem, p_send_sem, p_recv_sem,
+    local_sem, ring_send, ring_recv, a_send_sem, a_recv_sem, p_send_sem, p_recv_sem,
     y_send_sem, y_recv_sem, z_send_sem, z_recv_sem, word, ready, carried, help_recv, carry_send,
 ):
     b = lax.axis_index("blk")
@@ -258,8 +257,6 @@
     pass_on(2, (), (2, NZ - 2))
 
     text_out[...] = nt(pre_grad.astype(jnp.bfloat16), pert[...]).astype(jnp.bfloat16)
-    text_copy = pltpu.make_async_copy(text_out, text_grad_hbm, out_sem.at[0])
-    text_copy.start()
 
     for i in range(NX):
         for core in range(NC):
@@ -326,8 +323,6 @@
     image_dir = img * image_scale
     along_image = jnp.sum(image_dir * unit_image_grad, axis=1, keepdims=True)
     image_out[...] = (image_scale * (unit_image_grad - image_dir * along_image)).astype(jnp.bfloat16)
-    image_copy = pltpu.make_async_copy(image_out, image_grad_hbm, out_sem.at[1])
-    image_copy.start()
 
     block = z_send[z]
     for j, copy in sorted(zip(Z_ORDER, z_copies), key=lambda e: min(e[0], NZ - e[0])):
@@ -343,25 +338,17 @@
     def _():
         carry.wait_send()
 
-    text_copy.wait()
-    image_copy.wait()
-
-
-def placed(image_in, text_in, head_in, image_out, text_out, head_out, image, text, head, sem):
-    pairs = [(head_in, head, head_out)]
+
+def placed(image_in, text_in, head_in, image_out, text_out, head_out, sem):
+    copies = [pltpu.make_async_copy(head_in, head_out, sem.at[2 * PLACE_PARTS])]
     step = ROWS // PLACE_PARTS
     for n in range(PLACE_PARTS):
         rows = pl.ds(n * step, step)
-        pairs.append((image_in.at[rows], image.at[rows], image_out.at[rows]))
-        pairs.append((text_in.at[rows], text.at[rows], text_out.at[rows]))
-    reads = [pltpu.make_async_copy(a, b, sem.at[0, n]) for n, (a, b, _) in enumerate(pairs)]
-    writes = [pltpu.make_async_copy(b, c, sem.at[1, n]) for n, (_, b, c) in enumerate(pairs)]
-    for copy in reads:
-        copy.start()
-    for read, write in zip(reads, writes):
-        read.wait()
-        write.start()
-    for copy in writes:
+        copies.append(pltpu.make_async_copy(image_in.at[rows], image_out.at[rows], sem.at[2 * n]))
+        copies.append(pltpu.make_async_copy(text_in.at[rows], text_out.at[rows], sem.at[2 * n + 1]))
+    for copy in copies:
+        copy.start()
+    for copy in copies:
         copy.wait()
 
 
@@ -372,12 +359,12 @@
     results = pl.pallas_call(
         kernel,
         out_shape=(
-            jax.ShapeDtypeStruct((ROWS, D), bf16),
-            jax.ShapeDtypeStruct((ROWS, D), bf16),
-            jax.ShapeDtypeStruct((24, 36), f32),
+            pltpu.VMEM((ROWS, D), bf16),
+            pltpu.VMEM((ROWS, D), bf16),
+            pltpu.VMEM((24, 36), f32),
         ),
         in_specs=[any_spec] * 5 + [pl.BlockSpec(memory_space=pltpu.SMEM)] * 2,
-        out_specs=(any_spec, any_spec, pl.BlockSpec(memory_space=pltpu.VMEM)),
+        out_specs=(pl.BlockSpec(memory_space=pltpu.VMEM),) * 3,
         scratch_shapes=[
             pltpu.VMEM((2 * ROWS, D), bf16),
             pltpu.VMEM((2 * ROWS, D), bf16),
@@ -399,10 +386,7 @@
             pltpu.VMEM((NY, 96, 128), bf16),
             pltpu.VMEM((NZ, 8, 128), f32),
             pltpu.VMEM((NZ, 8, 128), f32),
-            pltpu.VMEM((ROWS, D), bf16),
-            pltpu.VMEM((ROWS, D), bf16),
             dma((4 + 2 * W_CHUNKS,)),
-            dma((2,)),
             dma((5,)),
             dma((5,)),
             dma((GROUP,)),
@@ -420,20 +404,19 @@
             dma,
         ],
         compiler_params=pltpu.CompilerParams(
-            collective_id=0, has_side_effects=True, vmem_limit_bytes=63 << 20
+            collective_id=0, has_side_effects=True, vmem_limit_bytes=56 << 20
         ),
         name="contrastive",
-    )(img, desc, ids.reshape(1, ROWS), w, dw, scale, bias)
+    )(*(pltpu.with_memory_space_constraint(v, pltpu.HBM) for v in (img, desc, ids.reshape(1, ROWS), w, dw)), scale, bias)
     return pl.pallas_call(
         placed,
         out_shape=[jax.ShapeDtypeStruct(r.shape, r.dtype) for r in results],
         in_specs=[any_spec] * 3,
         out_specs=[any_spec] * 3,
         scratch_shapes=[
-            *[pltpu.VMEM(r.shape, r.dtype) for r in results],
-            dma((2, 2 * PLACE_PARTS + 1)),
+            dma((2 * PLACE_PARTS + 1,)),
         ],
-        compiler_params=pltpu.CompilerParams(vmem_limit_bytes=63 << 20),
+        compiler_params=pltpu.CompilerParams(vmem_limit_bytes=4 << 20),
         name="placed",
     )(*results)
 

time: 51 us -> 49.2 us (0.965)
  Pallas kernels: 48.8 us -> 47.2 us
    pallas_call x1, Pallas kernels: 1.94 us -> 0.89 us  [shards(): pl.pallas_call(placed, out_shape=[jax.ShapeDtypeStruct(r.shape, r.dtype)...]
    pallas_call x1, Pallas kernels: 46.9 us -> 46.3 us  [shards(): pl.pallas_call(kernel, out_shape=(pltpu.VMEM((ROWS, D), bf16), pltpu.VMEM...]
where the time goes in v3:
time: 49.2 us; the launch traced here: 49.1 us
  Pallas kernels  47.2 us (96%)
  between operations  1.93 us (4%)
    pallas_call x1, Pallas kernels, shards(): pl.pallas_call(kernel, out_shape=(pltpu.VMEM((ROWS, D), bf16), pltpu.VMEM...  46.3 us

profile of v3, /device:TPU:1, one launch (start us, length us, event | category | flops | bytes accessed | tf_op | source)
XLA Modules:
  0.0 49.1 jit_solution(1490106428772602739)
XLA Ops:
  1.9 46.3 %contrastive.1 = (bf16[128,1152]{1,0:T(8,128)(2,1)S(1)}, bf16[128,1152]{1,0:T(8,128)(2,1)S(1)}, f32[24,36]{1,0:T(8,128)S(1)}) custom-call(bf16[128,1152]{1,0:T(8,128)(2,1)} %img_hbm.1, bf16[128,1152]{1,0:T(8,128)(2,1)} %desc_hbm.1, s32[1,128]{1,0:T(1,128)} %bitcast.1, bf16[1152,1152]{1,0:T(8,128)(2,1)} %w_hbm.1, bf16[1152,1152]{1,0:T(8,128)(2,1)} %dw_hbm.1, ...), custom_call_target="tpu_custom_call" | custom-call | tf_op jit(solution)/shard_map/contrastive/pallas_call | solution.py:359
  48.2 0.9 %placed.1 = (bf16[128,1152]{1,0:T(8,128)(2,1)}, bf16[128,1152]{1,0:T(8,128)(2,1)}, f32[24,36]{1,0:T(8,128)}) custom-call(bf16[128,1152]{1,0:T(8,128)(2,1)S(1)} %get-tuple-element.6.image_in, bf16[128,1152]{1,0:T(8,128)(2,1)S(1)} %get-tuple-element.7.text_in, f32[24,36]{1,0:T(8,128)S(1)} %get-tuple-element.8.head_in), custom_call_target="tpu_custom_call" | custom-call | tf_op jit(solution)/shard_map/placed/pallas_call | solution.py:411

commit v4 on v3

--- a/solution.py
+++ b/solution.py
@@ -15,7 +15,7 @@
 NX, NY, NZ, NC, ZL = 4, 8, 12, 2, 4
 GROUP = NX * NC
 W_CHUNKS = 3
-PLACE_PARTS = 4
+PLACE_PARTS = 2
 IMG_PARTS = ((0, 64), (64, 32), (96, 32))
 Y_ORDER = (4, 3, 5, 2, 6, 1, 7)
 Z_ORDER = (6, 5, 7, 4, 8, 3, 9, 2, 10, 1, 11)
@@ -148,11 +148,6 @@
         help_part(2, device_at(x, 1, z, 0)).start()
         send_img[0].start()
 
-    @pl.when(jnp.logical_not(goes_out))
-    def _():
-        for copy in send_img:
-            copy.start()
-
     def slot(i, core):
         return i * NC + core
 
@@ -165,6 +160,11 @@
         )
         copy.start()
         a_copies.append(copy)
+
+    @pl.when(jnp.logical_not(goes_out))
+    def _():
+        for copy in send_img:
+            copy.start()
 
     def a_arrived(s):
         return remote(at_send.at[0], at_all.at[s], a_send_sem.at[0], a_recv_sem.at[s], before)
@@ -258,17 +258,23 @@
 
     text_out[...] = nt(pre_grad.astype(jnp.bfloat16), pert[...]).astype(jnp.bfloat16)
 
-    for i in range(NX):
-        for core in range(NC):
-            if i in (1, 2, 3) and (i, core) not in ((NX - 1, 0), (1, 1)):
-                a_arrived(slot(i, core)).wait_recv()
-            if i:
-                p_arrived(slot(i, core)).wait_recv()
+    def product(slots):
+        features = jnp.concatenate([at_all[s] for s in slots], axis=1)
+        columns = jnp.concatenate([pt_all[s] for s in slots], axis=1)
+        return nt(features, columns)
+
     a_arrived(slot(0, 1 - c)).wait_recv()
     p_arrived(slot(0, 1 - c)).wait_recv()
-    features = jnp.concatenate([at_all[s] for s in range(GROUP)], axis=1)
-    columns = jnp.concatenate([pt_all[s] for s in range(GROUP)], axis=1)
-    r_buf[:, pl.ds(0, 144)] = nt(features, columns)
+    for i in (1, NX - 1):
+        for core in range(NC):
+            if (i, core) not in ((NX - 1, 0), (1, 1)):
+                a_arrived(slot(i, core)).wait_recv()
+            p_arrived(slot(i, core)).wait_recv()
+    r_buf[:, pl.ds(0, 144)] = product([slot(i, core) for i in (0, 1, NX - 1) for core in range(NC)])
+    for core in range(NC):
+        a_arrived(slot(2, core)).wait_recv()
+        p_arrived(slot(2, core)).wait_recv()
+    r_buf[:, pl.ds(0, 144)] += product([slot(2, core) for core in range(NC)])
     low = r_buf[:, pl.ds(0, 128)].reshape(24, 3, 8, 128)
     high = r_buf[:, pl.ds(128, 128)].reshape(24, 3, 8, 128)
     lane = lax.broadcasted_iota(jnp.int32, (24, 8, 128), 2)

time: 49.2 us -> 49 us (level)
  no operation moved by 1% of the time
where the time goes in v4:
time: 49 us; the launch traced here: 48.8 us
  Pallas kernels  46.9 us (96%)
  between operations  1.93 us (4%)
    pallas_call x1, Pallas kernels, shards(): pl.pallas_call(kernel, out_shape=(pltpu.VMEM((ROWS, D), bf16), pltpu.VMEM...  46 us

profile of v4, /device:TPU:1, one launch (start us, length us, event | category | flops | bytes accessed | tf_op | source)
XLA Modules:
  0.0 48.8 jit_solution(12309165793415872743)
XLA Ops:
  1.9 46.0 %contrastive.1 = (bf16[128,1152]{1,0:T(8,128)(2,1)S(1)}, bf16[128,1152]{1,0:T(8,128)(2,1)S(1)}, f32[24,36]{1,0:T(8,128)S(1)}) custom-call(bf16[128,1152]{1,0:T(8,128)(2,1)} %img_hbm.1, bf16[128,1152]{1,0:T(8,128)(2,1)} %desc_hbm.1, s32[1,128]{1,0:T(1,128)} %bitcast.1, bf16[1152,1152]{1,0:T(8,128)(2,1)} %w_hbm.1, bf16[1152,1152]{1,0:T(8,128)(2,1)} %dw_hbm.1, ...), custom_call_target="tpu_custom_call" | custom-call | tf_op jit(solution)/shard_map/contrastive/pallas_call | solution.py:365
  47.9 0.9 %placed.1 = (bf16[128,1152]{1,0:T(8,128)(2,1)}, bf16[128,1152]{1,0:T(8,128)(2,1)}, f32[24,36]{1,0:T(8,128)}) custom-call(bf16[128,1152]{1,0:T(8,128)(2,1)S(1)} %get-tuple-element.6.image_in, bf16[128,1152]{1,0:T(8,128)(2,1)S(1)} %get-tuple-element.7.text_in, f32[24,36]{1,0:T(8,128)S(1)} %get-tuple-element.8.head_in), custom_call_target="tpu_custom_call" | custom-call | tf_op jit(solution)/shard_map/placed/pallas_call | solution.py:417

commit v5 on v4

--- a/solution.py
+++ b/solution.py
@@ -61,6 +61,13 @@
     before = (lax.rem(b + 47, 48), d)
     group = [(i, f) for i in range(NX) for f in range(NC) if (i, f) != (0, 0)]
 
+    loads = [
+        pltpu.make_async_copy(desc_hbm, descs.at[pl.ds(0, ROWS)], local_sem.at[0]),
+        pltpu.make_async_copy(img_hbm, imgs.at[pl.ds(0, ROWS)], local_sem.at[1]),
+        pltpu.make_async_copy(ids_hbm, ids, local_sem.at[2]),
+    ]
+    loads[0].start()
+
     barrier = pltpu.get_barrier_semaphore()
     for i, f in group:
         pl.semaphore_signal(barrier, inc=1, device_id=device_at(x + i, y, z, c + f), device_id_type=MESH)
@@ -84,12 +91,7 @@
     for j in (1, NZ - 1):
         pl.semaphore_signal(barrier, inc=1, device_id=device_at(x, y, z + j, c), device_id_type=MESH)
 
-    loads = [
-        pltpu.make_async_copy(desc_hbm, descs.at[pl.ds(0, ROWS)], local_sem.at[0]),
-        pltpu.make_async_copy(img_hbm, imgs.at[pl.ds(0, ROWS)], local_sem.at[1]),
-        pltpu.make_async_copy(ids_hbm, ids, local_sem.at[2]),
-    ]
-    for copy in loads:
+    for copy in loads[1:]:
         copy.start()
     w_loads = []
     for n in range(W_CHUNKS):
@@ -122,7 +124,6 @@
                 word.at[2 * round_ + 1], inc=1, device_id=device_at(x, y, z + j, c), device_id_type=MESH
             )
 
-    pass_on(0, (1, NY - 1), (1, NZ - 1))
 
     def remote(src, dst, send, recv, device):
         return pltpu.make_async_remote_copy(
@@ -171,6 +172,8 @@
 
     def p_arrived(s):
         return remote(pt_send.at[0], pt_all.at[s], p_send_sem.at[0], p_recv_sem.at[s], before)
+
+    pass_on(0, (1, NY - 1), (1, NZ - 1))
 
     for n in range(W_CHUNKS):
         cols = pl.ds(n * WC, WC)

time: 49 us -> 49 us (level)
  no operation moved by 1% of the time
where the time goes in v5:
time: 49 us; the launch traced here: 48.8 us
  Pallas kernels  46.8 us (96%)
  between operations  1.93 us (4%)
    pallas_call x1, Pallas kernels, shards(): pl.pallas_call(kernel, out_shape=(pltpu.VMEM((ROWS, D), bf16), pltpu.VMEM...  46 us

profile of v5, /device:TPU:1, one launch (start us, length us, event | category | flops | bytes accessed | tf_op | source)
XLA Modules:
  0.0 48.8 jit_solution(8870147718061424463)
XLA Ops:
  1.9 46.0 %contrastive.1 = (bf16[128,1152]{1,0:T(8,128)(2,1)S(1)}, bf16[128,1152]{1,0:T(8,128)(2,1)S(1)}, f32[24,36]{1,0:T(8,128)S(1)}) custom-call(bf16[128,1152]{1,0:T(8,128)(2,1)} %img_hbm.1, bf16[128,1152]{1,0:T(8,128)(2,1)} %desc_hbm.1, s32[1,128]{1,0:T(1,128)} %bitcast.1, bf16[1152,1152]{1,0:T(8,128)(2,1)} %w_hbm.1, bf16[1152,1152]{1,0:T(8,128)(2,1)} %dw_hbm.1, ...), custom_call_target="tpu_custom_call" | custom-call | tf_op jit(solution)/shard_map/contrastive/pallas_call | solution.py:368
  47.9 0.9 %placed.1 = (bf16[128,1152]{1,0:T(8,128)(2,1)}, bf16[128,1152]{1,0:T(8,128)(2,1)}, f32[24,36]{1,0:T(8,128)}) custom-call(bf16[128,1152]{1,0:T(8,128)(2,1)S(1)} %get-tuple-element.6.image_in, bf16[128,1152]{1,0:T(8,128)(2,1)S(1)} %get-tuple-element.7.text_in, f32[24,36]{1,0:T(8,128)S(1)} %get-tuple-element.8.head_in), custom_call_target="tpu_custom_call" | custom-call | tf_op jit(solution)/shard_map/placed/pallas_call | solution.py:420
